TPU v7x, 32 devices: a whole 2x2x4 slice. The times are simulated.
32 devices in a mesh: groups: 2 (over y), energy: 4 (over z), tile: 2 (over x), mode: 2 (over core).
Axes of the slice: x: 2, y: 2, z: 4, core: 2. Of those that a mesh axis runs over, the one named last changes fastest.
Arguments:
- object_field: float32 [2, 16, 256, 192], P(None, ('groups', 'energy', 'mode'), 'tile'), parts along dimension 1, may hold values from -6 to 6
- probe_field: float32 [2, 3, 16, 128, 128], P(None, None, ('groups', 'energy', 'mode')), parts along dimension 2, may hold values from -6 to 6
- modulus: bfloat16 [16, 16, 128, 128], P(('groups', 'energy', 'mode'), 'tile'), parts along dimension 0, may hold values from 0 to 2
- offsets: int32 [32, 2], P(('groups', 'tile')), parts along dimension 0, may hold values from 0 to 31
- spectra_basis: float32 [8, 8], replicated, may hold values from -2 to 2
- analysis: float32 [8, 8], replicated, may hold values from -2 to 2
- threshold: float32 [8], replicated, may hold values from 0.05 to 0.5
Outputs:
- object_out: float32 [2, 16, 256, 192], P(None, ('groups', 'energy', 'mode'), 'tile'), parts along dimension 1
- probe_out: float32 [2, 3, 16, 128, 128], P(None, None, ('groups', 'energy', 'mode')), parts along dimension 2
There are 2 independent parts, one for each index of `groups`. A program takes and returns all parts, laid end to end along the dimension named above; an argument that names none is the same for every part. Nothing has to cross between parts.
All inputs are finite; a program needn't handle non-finite values.
Results may differ from a plain program's by a relative error of at most 0.0033.
Values may be sent and summed in bfloat16 or wider, within the bound.
A program may use at most 128 MiB of HBM per device.

v0:
```python
import functools
import math

import jax
import jax.numpy as jnp
import numpy as np
from jax import lax
from jax.experimental import pallas as pl
from jax.experimental.pallas import tpu as pltpu
from jax.sharding import PartitionSpec as P

PCOLS = 2
STEP = 32
MESH = pl.DeviceIdType.MESH
BF16 = jnp.bfloat16
F32 = jnp.float32


def dft_parts(extent):
    counter = np.arange(extent)
    phases = -2.0 * math.pi / extent * (counter[:, None] * counter[None, :] % extent)
    norm = 1.0 / math.sqrt(extent)
    cosine = (np.cos(phases) * norm).astype(np.float32)
    sine = (np.sin(phases) * norm).astype(np.float32)
    return np.concatenate([cosine, sine], axis=1).astype(jnp.bfloat16)


def dot(left, right):
    return jnp.dot(left, right, preferred_element_type=F32)


def kernel(
    sizes,
    off,
    basis,
    analysis,
    thr,
    dft,
    obj,
    probe,
    mod,
    out_obj,
    out_probe,
    fwd,
    bwd,
    ext,
    power,
    place,
    sum_n,
    sum_d,
    pn,
    pd,
    x_new,
    halo_out,
    halo_in,
    d_out,
    d_in,
    n_out,
    n_in,
    pn_all,
    pd_all,
    a_out,
    a_in,
    b_out,
    b_in,
    halo_sem,
    d_sem,
    n_sem,
    pn_send,
    pn_recv,
    pd_send,
    pd_recv,
    a_send,
    a_recv,
    b_send,
    b_recv,
):
    n_energy, n_mode, n_tile = sizes
    n_chan = n_energy * n_mode
    t = lax.axis_index("tile")
    me = lax.axis_index("energy") * n_mode + lax.axis_index("mode")
    modes, extent = probe.shape[1], probe.shape[2]
    rows, width = obj.shape[1], obj.shape[2]
    positions = mod.shape[0]
    lanes = ext.shape[3]
    pad_w = ext.shape[1] * lanes
    share = rows // n_chan
    comps = thr.shape[0]

    def tile_id(other):
        return {"tile": other}

    def chan_id(other):
        return {"energy": other // n_mode, "mode": other % n_mode}

    barrier = pltpu.get_barrier_semaphore()
    for step in range(1, n_chan):
        pl.semaphore_signal(
            barrier, inc=1, device_id=chan_id((me + step) % n_chan), device_id_type=MESH
        )
    for step in range(1, n_tile):
        pl.semaphore_signal(
            barrier, inc=1, device_id=tile_id((t + step) % n_tile), device_id_type=MESH
        )

    def fill(base, block):
        for start in range(0, width, lanes):
            part = min(lanes, width - start)
            ext[:, start // lanes, base : base + rows, :part] = block[
                :, :, start : start + part
            ].astype(F32)
            if part < lanes:
                ext[:, start // lanes, base : base + rows, part:] = jnp.zeros(
                    (2, rows, lanes - part), F32
                )

    def wide(ref, plane, at):
        return jnp.concatenate(
            [ref[plane, block, at] for block in range(pad_w // lanes)], axis=-1
        )

    rounded = obj[...].astype(BF16)
    halo_out[...] = rounded
    fill(0, rounded)

    pl.semaphore_wait(barrier, n_chan - 1 + n_tile - 1)

    def halo_copy():
        return pltpu.make_async_remote_copy(
            src_ref=halo_out,
            dst_ref=halo_in,
            send_sem=halo_sem.at[0],
            recv_sem=halo_sem.at[1],
            device_id=tile_id((t + n_tile - 1) % n_tile),
            device_id_type=MESH,
        )

    def down_copy(src, dst, sem):
        return pltpu.make_async_remote_copy(
            src_ref=src,
            dst_ref=dst,
            send_sem=sem.at[0],
            recv_sem=sem.at[1],
            device_id=tile_id((t + 1) % n_tile),
            device_id_type=MESH,
        )

    first = t == 0
    last = t == n_tile - 1

    @pl.when(jnp.logical_not(first))
    def _():
        halo_copy().start()

    cosine = dft[:, :extent]
    sine = dft[:, extent:]
    fwd[:extent, :extent] = cosine
    fwd[extent:, extent:] = cosine
    fwd[:extent, extent:] = -sine
    fwd[extent:, :extent] = sine
    bwd[:extent, :extent] = cosine
    bwd[extent:, extent:] = cosine
    bwd[:extent, extent:] = sine
    bwd[extent:, :extent] = -sine

    total = probe[0, 0] * probe[0, 0] + probe[1, 0] * probe[1, 0]
    for m in range(1, modes):
        total += probe[0, m] * probe[0, m] + probe[1, m] * probe[1, m]
    power[...] = total
    floor_d = 0.1 * jnp.max(total) + 1e-06

    place[...] = jnp.zeros_like(place)
    sum_n[...] = jnp.zeros_like(sum_n)
    sum_d[...] = jnp.zeros_like(sum_d)
    pn[...] = jnp.zeros_like(pn)
    pd[...] = jnp.zeros_like(pd)
    span = extent + STEP

    def widen(block, col):
        padded = jnp.concatenate([block, jnp.zeros((extent, pad_w - extent), F32)], axis=1)
        return pltpu.roll(padded, col, axis=1)

    def lay(plane, block, col):
        moved = widen(block, col)
        for start in range(0, pad_w, lanes):
            place[plane, start // lanes, STEP : STEP + extent] = moved[:, start : start + lanes]

    def put_power(q, carry):
        drop = off[q, 0]
        col = STEP * (q % PCOLS) + off[q, 1]
        base = pl.multiple_of(STEP * (q // PCOLS), STEP)
        lay(2, power[...], col)
        sum_d[pl.ds(base, span)] += wide(place, 2, pl.ds(STEP - drop, span))
        return carry

    lax.fori_loop(0, positions, put_power, 0)

    d_out[...] = sum_d[rows:, :width].astype(BF16)

    @pl.when(jnp.logical_not(last))
    def _():
        down_copy(d_out, d_in, d_sem).start()
        halo_copy().wait_recv()
        fill(rows, halo_in[...])

    @pl.when(last)
    def _():
        ext[:, :, rows:] = jnp.zeros((2, pad_w // lanes, rows, lanes), F32)

    def one(q, carry):
        drop = off[q, 0]
        col = STEP * (q % PCOLS) + off[q, 1]
        base = pl.multiple_of(STEP * (q // PCOLS), STEP)
        top = base + drop
        o_r = pltpu.roll(wide(ext, 0, pl.ds(top, extent)), lax.rem(pad_w - col, pad_w), axis=1)[:, :extent]
        o_i = pltpu.roll(wide(ext, 1, pl.ds(top, extent)), lax.rem(pad_w - col, pad_w), axis=1)[:, :extent]
        waves = []
        for m in range(modes):
            p_r, p_i = probe[0, m], probe[1, m]
            waves.append(
                jnp.concatenate([p_r * o_r - p_i * o_i, p_r * o_i + p_i * o_r], axis=0).astype(BF16)
            )
        half = dot(fwd[...], jnp.concatenate(waves, axis=1))
        cols = jnp.concatenate(
            [
                jnp.concatenate(
                    [
                        half[:extent, m * extent : (m + 1) * extent],
                        half[extent:, m * extent : (m + 1) * extent],
                    ],
                    axis=1,
                )
                for m in range(modes)
            ],
            axis=0,
        ).astype(BF16)
        spec = dot(cols, bwd[...])
        parts = [spec[m * extent : (m + 1) * extent] for m in range(modes)]
        squares = parts[0] * parts[0]
        for m in range(1, modes):
            squares += parts[m] * parts[m]
        mag = squares[:, :extent] + squares[:, extent:]
        factor = mod[q].astype(F32) * lax.rsqrt(mag + 0.01)
        both = jnp.concatenate([factor, factor], axis=1)
        scaled = jnp.concatenate([part * both for part in parts], axis=0).astype(BF16)
        ret = dot(scaled, fwd[...])
        stack = jnp.concatenate(
            [
                jnp.concatenate(
                    [
                        ret[m * extent : (m + 1) * extent, :extent],
                        ret[m * extent : (m + 1) * extent, extent:],
                    ],
                    axis=0,
                )
                for m in range(modes)
            ],
            axis=1,
        ).astype(BF16)
        wave = dot(bwd[...], stack)
        n_r = jnp.zeros((extent, extent), F32)
        n_i = jnp.zeros((extent, extent), F32)
        for m in range(modes):
            p_r, p_i = probe[0, m], probe[1, m]
            w_r = wave[:extent, m * extent : (m + 1) * extent]
            w_i = wave[extent:, m * extent : (m + 1) * extent]
            n_r += p_r * w_r + p_i * w_i
            n_i += p_r * w_i - p_i * w_r
            pn[0, m] += o_r * w_r + o_i * w_i
            pn[1, m] += o_r * w_i - o_i * w_r
        pd[...] += o_r * o_r + o_i * o_i
        lay(0, n_r, col)
        lay(1, n_i, col)
        for c in range(2):
            sum_n[c, pl.ds(base, span)] += wide(place, c, pl.ds(STEP - drop, span))
        return carry

    lax.fori_loop(0, positions, one, 0)

    for c in range(2):
        low = sum_n[c, rows:] - sum_d[rows:] * wide(ext, c, slice(rows, None))
        n_out[c] = low[:, :width].astype(BF16)

    @pl.when(jnp.logical_not(last))
    def _():
        down_copy(n_out, n_in, n_sem).start()

    pd_all[t] = pd[...].astype(BF16)
    pn_all[t] = (pn[...] - probe[...] * pd[...]).astype(BF16)

    def probe_copy(buffer, send, recv, step):
        return pltpu.make_async_remote_copy(
            src_ref=buffer.at[t],
            dst_ref=buffer.at[t],
            send_sem=send.at[step - 1],
            recv_sem=recv.at[step - 1],
            device_id=tile_id((t + step) % n_tile),
            device_id_type=MESH,
        )

    for step in range(1, n_tile):
        probe_copy(pd_all, pd_send, pd_recv, step).start()
        probe_copy(pn_all, pn_send, pn_recv, step).start()

    @pl.when(first)
    def _():
        n_in[...] = jnp.zeros_like(n_in)
        d_in[...] = jnp.zeros_like(d_in)

    @pl.when(jnp.logical_not(first))
    def _():
        down_copy(d_out, d_in, d_sem).wait_recv()
        down_copy(n_out, n_in, n_sem).wait_recv()

    d_top = sum_d[:rows, :width]
    n_top = sum_n[:, :rows, :width] - d_top[None] * obj[...].astype(BF16).astype(F32)
    n_top = n_top + n_in[...].astype(F32)
    d_top = d_top + d_in[...].astype(F32)
    fresh = obj[...] + n_top / (d_top + floor_d)[None]
    x_new[...] = fresh

    for block in range(n_chan):
        a_out[block, :, :share] = fresh[:, block * share : (block + 1) * share].astype(BF16)
    a_in[me] = a_out[me]

    def chan_copy(src, dst, send, recv, step):
        other = (me + step) % n_chan
        return pltpu.make_async_remote_copy(
            src_ref=src.at[other],
            dst_ref=dst.at[me],
            send_sem=send.at[step - 1],
            recv_sem=recv.at[step - 1],
            device_id=chan_id(other),
            device_id_type=MESH,
        )

    for step in range(1, n_chan):
        chan_copy(a_out, a_in, a_send, a_recv, step).start()
    for step in range(1, n_chan):
        chan_copy(a_out, a_in, a_send, a_recv, step).wait_recv()

    spectra = [a_in[e].astype(F32) for e in range(n_chan)]
    shrunk = []
    for k in range(comps):
        c = analysis[k, 0] * spectra[0]
        for e in range(1, n_chan):
            c += analysis[k, e] * spectra[e]
        limit = thr[k]
        shrunk.append(c - jnp.minimum(jnp.maximum(c, -limit), limit))
    for e in range(n_chan):
        x = basis[e, 0] * shrunk[0]
        for k in range(1, comps):
            x += basis[e, k] * shrunk[k]
        b_out[e] = x.astype(BF16)
    b_in[me] = b_out[me]

    for step in range(1, n_chan):
        chan_copy(b_out, b_in, b_send, b_recv, step).start()

    for step in range(1, n_tile):
        probe_copy(pd_all, pd_send, pd_recv, step).wait_recv()
        probe_copy(pn_all, pn_send, pn_recv, step).wait_recv()
    den = pd_all[0].astype(F32)
    num = pn_all[0].astype(F32)
    for other in range(1, n_tile):
        den += pd_all[other].astype(F32)
        num += pn_all[other].astype(F32)
    out_probe[...] = probe[...] + num / (den + 0.1 * jnp.max(den) + 1e-06)

    for step in range(1, n_chan):
        chan_copy(b_out, b_in, b_send, b_recv, step).wait_recv()
    for block in range(n_chan):
        at = slice(block * share, (block + 1) * share)
        out_obj[:, at] = 0.5 * x_new[:, at] + 0.5 * b_in[block, :, :share].astype(F32)

    @pl.when(jnp.logical_not(first))
    def _():
        halo_copy().wait_send()

    @pl.when(jnp.logical_not(last))
    def _():
        down_copy(d_out, d_in, d_sem).wait_send()
        down_copy(n_out, n_in, n_sem).wait_send()

    for step in range(1, n_tile):
        probe_copy(pd_all, pd_send, pd_recv, step).wait_send()
        probe_copy(pn_all, pn_send, pn_recv, step).wait_send()
    for step in range(1, n_chan):
        chan_copy(a_out, a_in, a_send, a_recv, step).wait_send()
        chan_copy(b_out, b_in, b_send, b_recv, step).wait_send()


def body(sizes, object_field, probe_field, modulus, offsets, spectra_basis, analysis, threshold):
    n_energy, n_mode, n_tile = sizes
    n_chan = n_energy * n_mode
    extent = probe_field.shape[-1]
    modes = probe_field.shape[1]
    rows, width = object_field.shape[2:]
    pad_w = -(-width // 128) * 128
    share = max(16, rows // n_chan)
    positions = offsets.shape[0]
    vmem = pl.BlockSpec(memory_space=pltpu.VMEM)
    smem = pl.BlockSpec(memory_space=pltpu.SMEM)
    dma = pltpu.SemaphoreType.DMA
    peers = max(1, n_tile - 1)
    flops = positions * modes * 4 * 2 * (2 * extent) ** 2 * extent
    out_obj, out_probe = pl.pallas_call(
        functools.partial(kernel, sizes),
        out_shape=(
            jax.ShapeDtypeStruct((2, rows, width), F32),
            jax.ShapeDtypeStruct((2, modes, extent, extent), F32),
        ),
        in_specs=[smem] * 4 + [vmem] * 4,
        out_specs=(vmem, vmem),
        scratch_shapes=[
            pltpu.VMEM((2 * extent, 2 * extent), BF16),
            pltpu.VMEM((2 * extent, 2 * extent), BF16),
            pltpu.VMEM((2, pad_w // 128, 2 * rows, 128), F32),
            pltpu.VMEM((extent, extent), F32),
            pltpu.VMEM((3, pad_w // 128, extent + 2 * STEP, 128), F32),
            pltpu.VMEM((2, 2 * rows, pad_w), F32),
            pltpu.VMEM((2 * rows, pad_w), F32),
            pltpu.VMEM((2, modes, extent, extent), F32),
            pltpu.VMEM((extent, extent), F32),
            pltpu.VMEM((2, rows, width), F32),
            pltpu.VMEM((2, rows, width), BF16),
            pltpu.VMEM((2, rows, width), BF16),
            pltpu.VMEM((rows, width), BF16),
            pltpu.VMEM((rows, width), BF16),
            pltpu.VMEM((2, rows, width), BF16),
            pltpu.VMEM((2, rows, width), BF16),
            pltpu.VMEM((n_tile, 2, modes, extent, extent), BF16),
            pltpu.VMEM((n_tile, extent, extent), BF16),
            pltpu.VMEM((n_chan, 2, share, width), BF16),
            pltpu.VMEM((n_chan, 2, share, width), BF16),
            pltpu.VMEM((n_chan, 2, share, width), BF16),
            pltpu.VMEM((n_chan, 2, share, width), BF16),
            dma((2,)),
            dma((2,)),
            dma((2,)),
            dma((peers,)),
            dma((peers,)),
            dma((peers,)),
            dma((peers,)),
            dma((n_chan - 1,)),
            dma((n_chan - 1,)),
            dma((n_chan - 1,)),
            dma((n_chan - 1,)),
        ],
        compiler_params=pltpu.CompilerParams(
            collective_id=0, has_side_effects=True, vmem_limit_bytes=40 * 1024 * 1024
        ),
        cost_estimate=pl.CostEstimate(flops=flops, bytes_accessed=2000000, transcendentals=0),
    )(
        offsets,
        spectra_basis,
        analysis,
        threshold,
        jnp.asarray(dft_parts(extent)),
        object_field.reshape(2, rows, width),
        probe_field.reshape(2, modes, extent, extent),
        modulus.reshape(positions, extent, extent),
    )
    return (out_obj[:, None], out_probe[:, :, None])


def solution(mesh):
    sizes = (mesh.shape["energy"], mesh.shape["mode"], mesh.shape["tile"])
    placed = (
        P(None, ("groups", "energy", "mode"), "tile", None),
        P(None, None, ("groups", "energy", "mode"), None, None),
        P(("groups", "energy", "mode"), "tile", None, None),
        P(("groups", "tile"), None),
        P(),
        P(),
        P(),
    )
    return jax.shard_map(
        functools.partial(body, sizes),
        mesh=mesh,
        in_specs=placed,
        out_specs=(
            P(None, ("groups", "energy", "mode"), "tile", None),
            P(None, None, ("groups", "energy", "mode"), None, None),
        ),
        check_vma=False,
    )
```

profile of v0, /device:TPU:3, one launch (start us, length us, event | category | flops | bytes accessed | tf_op | source)
XLA Modules:
  0.0 38.5 jit_solution(3547620995668295070)
XLA Ops:
  0.6 0.0 copy-start
  0.6 0.8 %copy.11.off = s32[8,2]{1,0:T(8,128)S(1)} copy(s32[8,2]{0,1:T(2,128)} %param.11) | data formatting | bytes 128 | tf_op args[3]
  1.4 0.0 copy-start.2
  1.4 0.0 copy-start.3
  1.4 0.0 copy-start.5
  1.4 1.1 %copy.10 = f32[2,1,128,192]{3,2,0,1:T(8,128)S(1)} copy(f32[2,1,128,192]{2,3,1,0:T(8,128)} %param.8) | data formatting | bytes 393216 | tf_op args[0]
  2.5 0.0 copy-start.4
  2.6 0.0 copy-done
  2.6 0.0 copy-done.2
  2.6 0.0 copy-done.3
  2.6 0.0 copy-done.5
  2.6 0.6 %copy-done.4 = f32[8]{0:T(128)S(1)} copy-done((f32[8]{0:T(128)S(1)}, f32[8]{0:T(128)}, u32[]{:S(2)}) %copy-start.4) | copy-done | bytes 56
  3.2 0.0 copy-start.1
  3.2 0.9 %copy-done.1 = bf16[1,8,128,128]{3,2,1,0:T(8,128)(2,1)S(1)} copy-done((bf16[1,8,128,128]{3,2,1,0:T(8,128)(2,1)S(1)}, bf16[1,8,128,128]{3,2,1,0:T(8,128)(2,1)}, u32[]{:S(2)}) %copy-start.1) | copy-done | bytes 262168
  4.2 32.8 %shard_map.95 = (f32[2,128,192]{2,1,0:T(8,128)S(1)}, f32[2,3,128,128]{3,2,1,0:T(8,128)S(1)}) custom-call(s32[8,2]{1,0:T(8,128)S(1)} %copy.11.off, f32[8,8]{1,0:T(8,128)S(1)} %copy-done.2, f32[8,8]{1,0:T(8,128)S(1)} %copy-done.3, f32[8]{0:T(128)S(1)} %copy-done.4, bf16[128,256]{1,0:T(8,128)(2,1)S(1)} %copy-done.5, f32[2,128,192]{2,1,0:T(8,128)S(1)} %bitcast.9, ...), custom_call_target="tpu_custom_call" | custom-call | flops 1610612736 | bytes 2000000 | tf_op jit(solution)/shard_map/pallas_call | solution.py:407
  37.0 0.8 %copy.12 = f32[2,1,128,192]{2,3,1,0:T(8,128)} copy(f32[2,1,128,192]{3,2,0,1:T(8,128)S(1)} %bitcast.8) | data formatting | bytes 393216
  37.8 0.7 %copy.15 = f32[2,3,1,128,128]{4,3,2,1,0:T(8,128)} copy(f32[2,3,1,128,128]{4,3,2,1,0:T(8,128)S(1)} %bitcast.7) | data formatting | bytes 786432
Async XLA Ops:
  0.6 1.9 %copy-start = (f32[2,3,1,128,128]{4,3,2,1,0:T(8,128)S(1)}, f32[2,3,1,128,128]{4,3,2,1,0:T(8,128)}, u32[]{:S(2)}) copy-start(f32[2,3,1,128,128]{4,3,2,1,0:T(8,128)} %param.9) | copy-start | bytes 1179652
  1.4 1.1 %copy-start.2 = (f32[8,8]{1,0:T(8,128)S(1)}, f32[8,8]{1,0:T(8,128)}, u32[]{:S(2)}) copy-start(f32[8,8]{1,0:T(8,128)} %basis.1) | copy-start | bytes 772
  1.4 1.1 %copy-start.3 = (f32[8,8]{1,0:T(8,128)S(1)}, f32[8,8]{1,0:T(8,128)}, u32[]{:S(2)}) copy-start(f32[8,8]{1,0:T(8,128)} %analysis.1) | copy-start | bytes 772
  1.4 1.1 %copy-start.5 = (bf16[128,256]{1,0:T(8,128)(2,1)S(1)}, bf16[128,256]{1,0:T(8,128)(2,1)}, u32[]{:S(2)}) copy-start(bf16[128,256]{1,0:T(8,128)(2,1)} %constant.2.clone.dft) | copy-start | bytes 196612
  2.5 0.7 %copy-start.4 = (f32[8]{0:T(128)S(1)}, f32[8]{0:T(128)}, u32[]{:S(2)}) copy-start(f32[8]{0:T(128)} %thr.1) | copy-start | bytes 100
  3.2 0.9 %copy-start.1 = (bf16[1,8,128,128]{3,2,1,0:T(8,128)(2,1)S(1)}, bf16[1,8,128,128]{3,2,1,0:T(8,128)(2,1)}, u32[]{:S(2)}) copy-start(bf16[1,8,128,128]{3,2,1,0:T(8,128)(2,1)} %param.10) | copy-start | bytes 786436
where the time goes:
time: 38.7 us; the launch traced here: 38.5 us
  Pallas kernels  32.8 us (85%)
  local copies, waits for them, and re-layouts  5.02 us (13%)
  between operations  0.7 us (2%)
    pallas_call x1, Pallas kernels, body(): pl.pallas_call(functools.partial(kernel, sizes), out_shape=(jax.ShapeDtyp...  32.8 us
    unnamed x16, local copies, waits for them, and re-layouts  5.02 us

commit v1 on v0

v1 whole, which is shorter than its diff:
```python
import functools
import math

import jax
import jax.numpy as jnp
import numpy as np
from jax import lax
from jax.experimental import pallas as pl
from jax.experimental.pallas import tpu as pltpu
from jax.sharding import PartitionSpec as P

PCOLS = 2
STEP = 32
MESH = pl.DeviceIdType.MESH
BF16 = jnp.bfloat16
F32 = jnp.float32


def dft_parts(extent):
    counter = np.arange(extent)
    phases = -2.0 * math.pi / extent * (counter[:, None] * counter[None, :] % extent)
    norm = 1.0 / math.sqrt(extent)
    cosine = (np.cos(phases) * norm).astype(np.float32)
    sine = (np.sin(phases) * norm).astype(np.float32)
    return np.concatenate([cosine, sine], axis=1).astype(jnp.bfloat16)


def dot(left, right):
    return jnp.dot(left, right, preferred_element_type=F32)


def kernel(
    sizes,
    off_hbm,
    basis_hbm,
    analysis_hbm,
    thr_hbm,
    dft_hbm,
    obj_hbm,
    probe_hbm,
    mod_hbm,
    out_obj,
    out_probe,
    off,
    basis,
    analysis,
    thr,
    dft,
    obj,
    probe,
    mod,
    load_sem,
    fwd,
    bwd,
    probe_t,
    ext,
    power,
    place,
    sum_n,
    sum_d,
    pn,
    pd,
    halo_out,
    halo_in,
    d_out,
    d_in,
    n_out,
    n_in,
    pn_all,
    pd_all,
    x_new,
    a_out,
    a_in,
    b_out,
    b_in,
    halo_sem,
    d_sem,
    n_sem,
    pn_send,
    pn_recv,
    pd_send,
    pd_recv,
    a_send,
    a_recv,
    b_send,
    b_recv,
):
    n_energy, n_mode, n_tile = sizes
    n_chan = n_energy * n_mode
    t = lax.axis_index("tile")
    me = lax.axis_index("energy") * n_mode + lax.axis_index("mode")
    modes, extent = probe.shape[1], probe.shape[2]
    width, rows = obj.shape[1], obj.shape[2]
    positions = mod.shape[0]
    share = width // n_chan
    used = 2 * share
    comps = thr.shape[0]

    def tile_id(other):
        return {"tile": other}

    def chan_id(other):
        return {"energy": other // n_mode, "mode": other % n_mode}

    barrier = pltpu.get_barrier_semaphore()
    for step in range(1, n_chan):
        pl.semaphore_signal(
            barrier, inc=1, device_id=chan_id((me + step) % n_chan), device_id_type=MESH
        )
    for step in range(1, n_tile):
        pl.semaphore_signal(
            barrier, inc=1, device_id=tile_id((t + step) % n_tile), device_id_type=MESH
        )

    pairs = [
        (obj_hbm, obj),
        (off_hbm, off),
        (probe_hbm, probe),
        (dft_hbm, dft),
        (mod_hbm, mod),
        (analysis_hbm, analysis),
        (basis_hbm, basis),
        (thr_hbm, thr),
    ]
    loads = [
        pltpu.make_async_copy(src, dst, load_sem.at[i]) for i, (src, dst) in enumerate(pairs)
    ]
    for load in loads:
        load.start()

    place[...] = jnp.zeros_like(place)
    sum_n[...] = jnp.zeros_like(sum_n)
    sum_d[...] = jnp.zeros_like(sum_d)
    pn[...] = jnp.zeros_like(pn)
    pd[...] = jnp.zeros_like(pd)

    loads[0].wait()
    rounded = obj[...].astype(BF16)
    halo_out[...] = rounded
    ext[:, 0] = rounded.astype(F32)

    pl.semaphore_wait(barrier, n_chan - 1 + n_tile - 1)

    def halo_copy():
        return pltpu.make_async_remote_copy(
            src_ref=halo_out,
            dst_ref=halo_in,
            send_sem=halo_sem.at[0],
            recv_sem=halo_sem.at[1],
            device_id=tile_id((t + n_tile - 1) % n_tile),
            device_id_type=MESH,
        )

    def down_copy(src, dst, sem):
        return pltpu.make_async_remote_copy(
            src_ref=src,
            dst_ref=dst,
            send_sem=sem.at[0],
            recv_sem=sem.at[1],
            device_id=tile_id((t + 1) % n_tile),
            device_id_type=MESH,
        )

    first = t == 0
    last = t == n_tile - 1

    @pl.when(jnp.logical_not(first))
    def _():
        halo_copy().start()

    loads[2].wait()
    total = jnp.zeros((extent, extent), F32)
    for m in range(modes):
        for c in range(2):
            turned = probe[c, m].T
            probe_t[c, m] = turned
            total += turned * turned
    power[...] = total
    floor_d = 0.1 * jnp.max(total) + 1e-06
    span = extent + STEP

    def lay(plane, block, row):
        moved = pltpu.roll(
            jnp.concatenate([block, jnp.zeros((extent, rows), F32)], axis=1), row, axis=1
        )
        place[plane, 0, STEP : STEP + extent] = moved[:, :rows]
        place[plane, 1, STEP : STEP + extent] = moved[:, rows:]

    loads[1].wait()

    def put_power(k, carry):
        for c in range(PCOLS):
            q = k * PCOLS + c
            lay(c, power[...], STEP * k + off[0, q])
            for b in range(2):
                sum_d[b, STEP * c : STEP * c + span] += place[
                    c, b, pl.ds(STEP - off[1, q], span)
                ]
        return carry

    lax.fori_loop(0, positions // PCOLS, put_power, 0)

    d_out[...] = sum_d[1].astype(BF16)

    loads[3].wait()
    cosine = dft[:, :extent]
    sine = dft[:, extent:]
    fwd[:extent, :extent] = cosine
    fwd[extent:, extent:] = cosine
    fwd[:extent, extent:] = -sine
    fwd[extent:, :extent] = sine
    bwd[:extent, :extent] = cosine
    bwd[extent:, extent:] = cosine
    bwd[:extent, extent:] = sine
    bwd[extent:, :extent] = -sine
    loads[4].wait()

    @pl.when(jnp.logical_not(last))
    def _():
        down_copy(d_out, d_in, d_sem).start()
        halo_copy().wait_recv()
        ext[:, 1] = halo_in[...].astype(F32)

    @pl.when(last)
    def _():
        ext[:, 1] = jnp.zeros((2, width, rows), F32)

    def window(plane, row, col):
        both = jnp.concatenate(
            [ext[plane, b, pl.ds(col, extent)] for b in range(2)], axis=1
        )
        return pltpu.roll(both, lax.rem(2 * rows - row, 2 * rows), axis=1)[:, :extent]

    def lanes_of(array, index):
        return array[:, index * extent : (index + 1) * extent]

    def rows_of(array, index):
        return array[index * extent : (index + 1) * extent]

    def one(k, carry):
        objects, tall = [], []
        for c in range(PCOLS):
            q = k * PCOLS + c
            row, col = STEP * k + off[0, q], STEP * c + off[1, q]
            o_r, o_i = window(0, row, col), window(1, row, col)
            objects.append((o_r, o_i))
            for m in range(modes):
                p_r, p_i = probe_t[0, m], probe_t[1, m]
                tall.append(
                    jnp.concatenate(
                        [p_r * o_r - p_i * o_i, p_r * o_i + p_i * o_r], axis=1
                    ).astype(BF16)
                )
        n_c = []
        for c in range(PCOLS):
            half = dot(jnp.concatenate(tall[c * modes : (c + 1) * modes], axis=0), bwd[...])
            wide = jnp.concatenate(
                [
                    jnp.concatenate(
                        [rows_of(half, m)[:, :extent], rows_of(half, m)[:, extent:]], axis=0
                    )
                    for m in range(modes)
                ],
                axis=1,
            ).astype(BF16)
            spec = dot(fwd[...], wide)
            squares = lanes_of(spec, 0) * lanes_of(spec, 0)
            for m in range(1, modes):
                squares += lanes_of(spec, m) * lanes_of(spec, m)
            mag = squares[:extent] + squares[extent:]
            factor = mod[k * PCOLS + c].astype(F32).T * lax.rsqrt(mag + 0.01)
            both = jnp.concatenate([factor, factor], axis=0)
            scaled = jnp.concatenate(
                [(lanes_of(spec, m) * both).astype(BF16) for m in range(modes)], axis=1
            )
            ret = dot(bwd[...], scaled)
            cols = jnp.concatenate(
                [
                    jnp.concatenate(
                        [lanes_of(ret, m)[:extent], lanes_of(ret, m)[extent:]], axis=1
                    )
                    for m in range(modes)
                ],
                axis=0,
            ).astype(BF16)
            wave = dot(cols, fwd[...])
            o_r, o_i = objects[c]
            n_r = jnp.zeros((extent, extent), F32)
            n_i = jnp.zeros((extent, extent), F32)
            for m in range(modes):
                p_r, p_i = probe_t[0, m], probe_t[1, m]
                w_r, w_i = rows_of(wave, m)[:, :extent], rows_of(wave, m)[:, extent:]
                n_r += p_r * w_r + p_i * w_i
                n_i += p_r * w_i - p_i * w_r
                pn[0, m] += o_r * w_r + o_i * w_i
                pn[1, m] += o_r * w_i - o_i * w_r
            pd[...] += o_r * o_r + o_i * o_i
            n_c.append((n_r, n_i))
        for c in range(PCOLS):
            q = k * PCOLS + c
            for plane in range(2):
                lay(2 * c + plane, n_c[c][plane], STEP * k + off[0, q])
        for c in range(PCOLS):
            q = k * PCOLS + c
            for plane in range(2):
                for b in range(2):
                    sum_n[plane, b, STEP * c : STEP * c + span] += place[
                        2 * c + plane, b, pl.ds(STEP - off[1, q], span)
                    ]
        return carry

    lax.fori_loop(0, positions // PCOLS, one, 0)

    for plane in range(2):
        n_out[plane] = (sum_n[plane, 1] - sum_d[1] * ext[plane, 1]).astype(BF16)

    @pl.when(jnp.logical_not(last))
    def _():
        down_copy(n_out, n_in, n_sem).start()

    pd_all[t] = pd[...].astype(BF16)
    pn_all[t] = (pn[...] - probe_t[...] * pd[...]).astype(BF16)

    def probe_copy(buffer, send, recv, step):
        return pltpu.make_async_remote_copy(
            src_ref=buffer.at[t],
            dst_ref=buffer.at[t],
            send_sem=send.at[step - 1],
            recv_sem=recv.at[step - 1],
            device_id=tile_id((t + step) % n_tile),
            device_id_type=MESH,
        )

    for step in range(1, n_tile):
        probe_copy(pd_all, pd_send, pd_recv, step).start()
        probe_copy(pn_all, pn_send, pn_recv, step).start()

    @pl.when(first)
    def _():
        n_in[...] = jnp.zeros_like(n_in)
        d_in[...] = jnp.zeros_like(d_in)

    @pl.when(jnp.logical_not(first))
    def _():
        down_copy(d_out, d_in, d_sem).wait_recv()
        down_copy(n_out, n_in, n_sem).wait_recv()

    scale = 1.0 / (sum_d[0] + d_in[...].astype(F32) + floor_d)
    for plane in range(2):
        top = sum_n[plane, 0] - sum_d[0] * ext[plane, 0] + n_in[plane].astype(F32)
        x_new[plane] = obj[plane] + top * scale

    for block in range(n_chan):
        at = slice(block * share, (block + 1) * share)
        a_out[block, :used] = jnp.concatenate([x_new[0, at], x_new[1, at]], axis=0).astype(BF16)

    def chan_copy(src, dst, send, recv, step):
        other = (me + step) % n_chan
        return pltpu.make_async_remote_copy(
            src_ref=src.at[other],
            dst_ref=dst.at[me],
            send_sem=send.at[step - 1],
            recv_sem=recv.at[step - 1],
            device_id=chan_id(other),
            device_id_type=MESH,
        )

    for step in range(1, n_chan):
        chan_copy(a_out, a_in, a_send, a_recv, step).start()
    a_in[me] = a_out[me]
    for i in range(5, 8):
        loads[i].wait()
    for step in range(1, n_chan):
        chan_copy(a_out, a_in, a_send, a_recv, step).wait_recv()

    spectra = [a_in[e].astype(F32) for e in range(n_chan)]
    shrunk = []
    for k in range(comps):
        c = analysis[k, 0] * spectra[0]
        for e in range(1, n_chan):
            c += analysis[k, e] * spectra[e]
        limit = thr[k]
        shrunk.append(c - jnp.minimum(jnp.maximum(c, -limit), limit))
    for e in range(n_chan):
        x = basis[e, 0] * shrunk[0]
        for k in range(1, comps):
            x += basis[e, k] * shrunk[k]
        b_out[e] = x.astype(BF16)

    for step in range(1, n_chan):
        chan_copy(b_out, b_in, b_send, b_recv, step).start()
    b_in[me] = b_out[me]

    for step in range(1, n_tile):
        probe_copy(pd_all, pd_send, pd_recv, step).wait_recv()
        probe_copy(pn_all, pn_send, pn_recv, step).wait_recv()
    den = pd_all[0].astype(F32)
    for other in range(1, n_tile):
        den += pd_all[other].astype(F32)
    scale = 1.0 / (den + 0.1 * jnp.max(den) + 1e-06)
    for c in range(2):
        for m in range(modes):
            num = pn_all[0, c, m].astype(F32)
            for other in range(1, n_tile):
                num += pn_all[other, c, m].astype(F32)
            out_probe[c, m] = probe[c, m] + (num * scale).T

    for step in range(1, n_chan):
        chan_copy(b_out, b_in, b_send, b_recv, step).wait_recv()
    for block in range(n_chan):
        at = slice(block * share, (block + 1) * share)
        back = b_in[block].astype(F32)
        out_obj[0, at] = 0.5 * x_new[0, at] + 0.5 * back[:share]
        out_obj[1, at] = 0.5 * x_new[1, at] + 0.5 * back[share:used]

    @pl.when(jnp.logical_not(first))
    def _():
        halo_copy().wait_send()

    @pl.when(jnp.logical_not(last))
    def _():
        down_copy(d_out, d_in, d_sem).wait_send()
        down_copy(n_out, n_in, n_sem).wait_send()

    for step in range(1, n_tile):
        probe_copy(pd_all, pd_send, pd_recv, step).wait_send()
        probe_copy(pn_all, pn_send, pn_recv, step).wait_send()
    for step in range(1, n_chan):
        chan_copy(a_out, a_in, a_send, a_recv, step).wait_send()
        chan_copy(b_out, b_in, b_send, b_recv, step).wait_send()


def body(sizes, object_field, probe_field, modulus, offsets, spectra_basis, analysis, threshold):
    n_energy, n_mode, n_tile = sizes
    n_chan = n_energy * n_mode
    extent = probe_field.shape[-1]
    modes = probe_field.shape[1]
    rows, width = object_field.shape[2:]
    share = -(-2 * (width // n_chan) // 16) * 16
    positions = offsets.shape[0]
    hbm = pl.BlockSpec(memory_space=pltpu.HBM)
    vmem = pl.BlockSpec(memory_space=pltpu.VMEM)
    dma = pltpu.SemaphoreType.DMA
    peers = max(1, n_tile - 1)
    flops = positions * modes * 4 * 2 * (2 * extent) ** 2 * extent
    dft = dft_parts(extent)
    out_obj, out_probe = pl.pallas_call(
        functools.partial(kernel, sizes),
        out_shape=(
            jax.ShapeDtypeStruct((2, width, rows), F32),
            jax.ShapeDtypeStruct((2, modes, extent, extent), F32),
        ),
        in_specs=[hbm] * 8,
        out_specs=(vmem, vmem),
        scratch_shapes=[
            pltpu.SMEM(offsets.shape[::-1], jnp.int32),
            pltpu.SMEM(spectra_basis.shape, F32),
            pltpu.SMEM(analysis.shape, F32),
            pltpu.SMEM(threshold.shape, F32),
            pltpu.VMEM(dft.shape, BF16),
            pltpu.VMEM((2, width, rows), F32),
            pltpu.VMEM((2, modes, extent, extent), F32),
            pltpu.VMEM((positions, extent, extent), BF16),
            dma((8,)),
            pltpu.VMEM((2 * extent, 2 * extent), BF16),
            pltpu.VMEM((2 * extent, 2 * extent), BF16),
            pltpu.VMEM((2, modes, extent, extent), F32),
            pltpu.VMEM((2, 2, width, rows), F32),
            pltpu.VMEM((extent, extent), F32),
            pltpu.VMEM((2 * PCOLS, 2, extent + 2 * STEP, rows), F32),
            pltpu.VMEM((2, 2, width, rows), F32),
            pltpu.VMEM((2, width, rows), F32),
            pltpu.VMEM((2, modes, extent, extent), F32),
            pltpu.VMEM((extent, extent), F32),
            pltpu.VMEM((2, width, rows), BF16),
            pltpu.VMEM((2, width, rows), BF16),
            pltpu.VMEM((width, rows), BF16),
            pltpu.VMEM((width, rows), BF16),
            pltpu.VMEM((2, width, rows), BF16),
            pltpu.VMEM((2, width, rows), BF16),
            pltpu.VMEM((n_tile, 2, modes, extent, extent), BF16),
            pltpu.VMEM((n_tile, extent, extent), BF16),
            pltpu.VMEM((2, width, rows), F32),
            pltpu.VMEM((n_chan, share, rows), BF16),
            pltpu.VMEM((n_chan, share, rows), BF16),
            pltpu.VMEM((n_chan, share, rows), BF16),
            pltpu.VMEM((n_chan, share, rows), BF16),
            dma((2,)),
            dma((2,)),
            dma((2,)),
            dma((peers,)),
            dma((peers,)),
            dma((peers,)),
            dma((peers,)),
            dma((n_chan - 1,)),
            dma((n_chan - 1,)),
            dma((n_chan - 1,)),
            dma((n_chan - 1,)),
        ],
        compiler_params=pltpu.CompilerParams(
            collective_id=0, has_side_effects=True, vmem_limit_bytes=40 * 1024 * 1024
        ),
        cost_estimate=pl.CostEstimate(flops=flops, bytes_accessed=2000000, transcendentals=0),
    )(
        offsets.T,
        spectra_basis,
        analysis,
        threshold,
        jnp.asarray(dft),
        jnp.swapaxes(object_field, 2, 3).reshape(2, width, rows),
        probe_field.reshape(2, modes, extent, extent),
        modulus.reshape(positions, extent, extent),
    )
    return (jnp.swapaxes(out_obj, 1, 2)[:, None], out_probe[:, :, None])


def solution(mesh):
    sizes = (mesh.shape["energy"], mesh.shape["mode"], mesh.shape["tile"])
    placed = (
        P(None, ("groups", "energy", "mode"), "tile", None),
        P(None, None, ("groups", "energy", "mode"), None, None),
        P(("groups", "energy", "mode"), "tile", None, None),
        P(("groups", "tile"), None),
        P(),
        P(),
        P(),
    )
    return jax.shard_map(
        functools.partial(body, sizes),
        mesh=mesh,
        in_specs=placed,
        out_specs=(
            P(None, ("groups", "energy", "mode"), "tile", None),
            P(None, None, ("groups", "energy", "mode"), None, None),
        ),
        check_vma=False,
    )
```

time: 38.7 us -> 35.4 us (0.915)
  Pallas kernels: 32.8 us -> 27.9 us
  local copies, waits for them, and re-layouts: 5.02 us -> 6.5 us
    pallas_call x1, Pallas kernels: 32.8 us -> 27.9 us  [body(): pl.pallas_call(functools.partial(kernel, sizes), out_shape=(jax.ShapeDtyp...]
    unnamed x16 -> x18, local copies, waits for them, and re-layouts: 5.02 us -> 6.5 us
where the time goes in v1:
time: 35.4 us; the launch traced here: 35 us
  Pallas kernels  27.9 us (79%)
  local copies, waits for them, and re-layouts  6.5 us (18%)
  between operations  0.67 us (2%)
    pallas_call x1, Pallas kernels, body(): pl.pallas_call(functools.partial(kernel, sizes), out_shape=(jax.ShapeDtyp...  27.9 us
    unnamed x18, local copies, waits for them, and re-layouts  6.5 us

profile of v1, /device:TPU:3, one launch (start us, length us, event | category | flops | bytes accessed | tf_op | source)
XLA Modules:
  0.0 35.0 jit_solution(17910395977685939335)
XLA Ops:
  0.6 0.0 copy-start.3
  0.6 0.0 copy-start.5
  0.7 0.0 copy-start.6
  0.7 0.7 %copy-done.3 = f32[8,8]{1,0:T(8,128)S(1)} copy-done((f32[8,8]{1,0:T(8,128)S(1)}, f32[8,8]{1,0:T(8,128)}, u32[]{:S(2)}) %copy-start.3) | copy-done | bytes 280
  1.3 0.0 copy-done.5
  1.3 0.0 copy-done.6
  1.3 0.0 copy-start
  1.3 1.0 %copy-done = f32[2,3,1,128,128]{4,3,2,1,0:T(8,128)S(1)} copy-done((f32[2,3,1,128,128]{4,3,2,1,0:T(8,128)S(1)}, f32[2,3,1,128,128]{4,3,2,1,0:T(8,128)}, u32[]{:S(2)}) %copy-start) | copy-done | bytes 393240
  2.3 0.0 copy-start.1
  2.3 0.9 %copy-done.1 = bf16[1,8,128,128]{3,2,1,0:T(8,128)(2,1)S(1)} copy-done((bf16[1,8,128,128]{3,2,1,0:T(8,128)(2,1)S(1)}, bf16[1,8,128,128]{3,2,1,0:T(8,128)(2,1)}, u32[]{:S(2)}) %copy-start.1) | copy-done | bytes 262168
  3.3 0.0 copy-start.2
  3.3 0.9 %copy-done.2 = f32[2,1,128,192]{2,3,1,0:T(8,128)S(1)} copy-done((f32[2,1,128,192]{2,3,1,0:T(8,128)S(1)}, f32[2,1,128,192]{2,3,1,0:T(8,128)}, u32[]{:S(2)}) %copy-start.2) | copy-done | bytes 196632
  4.2 0.0 copy-start.4
  4.2 0.7 %copy-done.4 = f32[8,8]{1,0:T(8,128)S(1)} copy-done((f32[8,8]{1,0:T(8,128)S(1)}, f32[8,8]{1,0:T(8,128)}, u32[]{:S(2)}) %copy-start.4) | copy-done | bytes 280
  4.9 0.0 copy-start.7
  4.9 0.8 %copy-done.7 = bf16[128,256]{1,0:T(8,128)(2,1)S(1)} copy-done((bf16[128,256]{1,0:T(8,128)(2,1)S(1)}, bf16[128,256]{1,0:T(8,128)(2,1)}, u32[]{:S(2)}) %copy-start.7) | copy-done | bytes 65560
  5.7 27.9 %shard_map.95 = (f32[2,192,128]{2,1,0:T(8,128)S(1)}, f32[2,3,128,128]{3,2,1,0:T(8,128)S(1)}) custom-call(s32[2,8]{1,0:T(2,128)S(1)} %bitcast.21, f32[8,8]{1,0:T(8,128)S(1)} %copy-done.3, f32[8,8]{1,0:T(8,128)S(1)} %copy-done.4, f32[8]{0:T(128)S(1)} %copy-done.6, bf16[128,256]{1,0:T(8,128)(2,1)S(1)} %copy-done.7, f32[2,192,128]{2,1,0:T(8,128)S(1)} %bitcast.20, ...), custom_call_target="tpu_custom_call" | custom-call | flops 1610612736 | bytes 2000000 | tf_op jit(solution)/shard_map/pallas_call | solution.py:447
  33.6 0.7 %copy.15 = f32[2,1,128,192]{2,3,1,0:T(8,128)} copy(f32[2,1,128,192]{2,3,1,0:T(8,128)S(1)} %bitcast.17) | data formatting | bytes 393216
  34.3 0.7 %copy.16 = f32[2,3,1,128,128]{4,3,2,1,0:T(8,128)} copy(f32[2,3,1,128,128]{4,3,2,1,0:T(8,128)S(1)} %bitcast.16) | data formatting | bytes 786432
Async XLA Ops:
  0.6 0.7 %copy-start.3 = (f32[8,8]{1,0:T(8,128)S(1)}, f32[8,8]{1,0:T(8,128)}, u32[]{:S(2)}) copy-start(f32[8,8]{1,0:T(8,128)} %basis_hbm.1) | copy-start | bytes 772
  0.6 0.7 %copy-start.5 = (s32[8,2]{0,1:T(2,128)S(1)}, s32[8,2]{0,1:T(2,128)}, u32[]{:S(2)}) copy-start(s32[8,2]{0,1:T(2,128)} %param.11) | copy-start | bytes 196
  0.7 0.7 %copy-start.6 = (f32[8]{0:T(128)S(1)}, f32[8]{0:T(128)}, u32[]{:S(2)}) copy-start(f32[8]{0:T(128)} %thr_hbm.1) | copy-start | bytes 100
  1.3 1.0 %copy-start = (f32[2,3,1,128,128]{4,3,2,1,0:T(8,128)S(1)}, f32[2,3,1,128,128]{4,3,2,1,0:T(8,128)}, u32[]{:S(2)}) copy-start(f32[2,3,1,128,128]{4,3,2,1,0:T(8,128)} %param.9) | copy-start | bytes 1179652
  2.3 0.9 %copy-start.1 = (bf16[1,8,128,128]{3,2,1,0:T(8,128)(2,1)S(1)}, bf16[1,8,128,128]{3,2,1,0:T(8,128)(2,1)}, u32[]{:S(2)}) copy-start(bf16[1,8,128,128]{3,2,1,0:T(8,128)(2,1)} %param.10) | copy-start | bytes 786436
  3.3 0.9 %copy-start.2 = (f32[2,1,128,192]{2,3,1,0:T(8,128)S(1)}, f32[2,1,128,192]{2,3,1,0:T(8,128)}, u32[]{:S(2)}) copy-start(f32[2,1,128,192]{2,3,1,0:T(8,128)} %param.8) | copy-start | bytes 589828
  4.2 0.7 %copy-start.4 = (f32[8,8]{1,0:T(8,128)S(1)}, f32[8,8]{1,0:T(8,128)}, u32[]{:S(2)}) copy-start(f32[8,8]{1,0:T(8,128)} %analysis_hbm.1) | copy-start | bytes 772
  4.9 0.8 %copy-start.7 = (bf16[128,256]{1,0:T(8,128)(2,1)S(1)}, bf16[128,256]{1,0:T(8,128)(2,1)}, u32[]{:S(2)}) copy-start(bf16[128,256]{1,0:T(8,128)(2,1)} %constant.2.clone.dft_hbm) | copy-start | bytes 196612

commit v2 on v1

--- a/solution.py
+++ b/solution.py
@@ -66,6 +66,8 @@
     d_in,
     n_out,
     n_in,
+    rest_out,
+    rest_in,
     pn_all,
     pd_all,
     x_new,
@@ -135,28 +137,35 @@
     pd[...] = jnp.zeros_like(pd)
 
     loads[0].wait()
-    rounded = obj[...].astype(BF16)
-    halo_out[...] = rounded
-    ext[:, 0] = rounded.astype(F32)
+    near, fold = width // 2, rows // 2
+    for part in range(2):
+        halo_out[part] = jnp.concatenate(
+            [
+                obj[:, :near, part * fold : (part + 1) * fold],
+                obj[:, near:, part * fold : (part + 1) * fold],
+            ],
+            axis=2,
+        ).astype(BF16)
+    ext[:, 0] = obj[...].astype(BF16).astype(F32)
 
     pl.semaphore_wait(barrier, n_chan - 1 + n_tile - 1)
 
-    def halo_copy():
+    def halo_copy(part):
         return pltpu.make_async_remote_copy(
-            src_ref=halo_out,
-            dst_ref=halo_in,
-            send_sem=halo_sem.at[0],
-            recv_sem=halo_sem.at[1],
+            src_ref=halo_out.at[part],
+            dst_ref=halo_in.at[part],
+            send_sem=halo_sem.at[part],
+            recv_sem=halo_sem.at[2 + part],
             device_id=tile_id((t + n_tile - 1) % n_tile),
             device_id_type=MESH,
         )
 
-    def down_copy(src, dst, sem):
+    def down_copy(src, dst, send, recv):
         return pltpu.make_async_remote_copy(
             src_ref=src,
             dst_ref=dst,
-            send_sem=sem.at[0],
-            recv_sem=sem.at[1],
+            send_sem=send,
+            recv_sem=recv,
             device_id=tile_id((t + 1) % n_tile),
             device_id_type=MESH,
         )
@@ -166,7 +175,8 @@
 
     @pl.when(jnp.logical_not(first))
     def _():
-        halo_copy().start()
+        halo_copy(0).start()
+        halo_copy(1).start()
 
     loads[2].wait()
     total = jnp.zeros((extent, extent), F32)
@@ -215,11 +225,16 @@
     bwd[extent:, :extent] = -sine
     loads[4].wait()
 
+    def take_halo(part):
+        halo_copy(part).wait_recv()
+        packed = halo_in[part].astype(F32)
+        ext[:, 1, :near, part * fold : (part + 1) * fold] = packed[:, :, :fold]
+        ext[:, 1, near:, part * fold : (part + 1) * fold] = packed[:, :, fold:]
+
     @pl.when(jnp.logical_not(last))
     def _():
-        down_copy(d_out, d_in, d_sem).start()
-        halo_copy().wait_recv()
-        ext[:, 1] = halo_in[...].astype(F32)
+        down_copy(d_out, d_in, d_sem.at[0], d_sem.at[1]).start()
+        take_halo(0)
 
     @pl.when(last)
     def _():
@@ -237,7 +252,29 @@
     def rows_of(array, index):
         return array[index * extent : (index + 1) * extent]
 
-    def one(k, carry):
+    turns = positions // PCOLS
+    group = width // (rows // STEP)
+
+    def send_most():
+        for plane in range(2):
+            n_out[plane] = (sum_n[plane, 1] - sum_d[1] * ext[plane, 1]).astype(BF16)
+            sum_n[plane, 1] = jnp.zeros((width, rows), F32)
+
+        @pl.when(jnp.logical_not(last))
+        def _():
+            down_copy(n_out, n_in, n_sem.at[0], n_sem.at[1]).start()
+
+    def one(i, carry):
+        k = lax.rem(i + 1, turns)
+
+        @pl.when(jnp.logical_and(i == 1, jnp.logical_not(last)))
+        def _():
+            take_halo(1)
+
+        @pl.when(i == turns - 1)
+        def _():
+            send_most()
+
         objects, tall = [], []
         for c in range(PCOLS):
             q = k * PCOLS + c
@@ -309,45 +346,41 @@
                     ]
         return carry
 
-    lax.fori_loop(0, positions // PCOLS, one, 0)
+    lax.fori_loop(0, turns, one, 0)
 
     for plane in range(2):
-        n_out[plane] = (sum_n[plane, 1] - sum_d[1] * ext[plane, 1]).astype(BF16)
+        rest_out[plane] = jnp.concatenate(
+            [
+                sum_n[plane, 1, g * group : (g + 1) * group, :STEP]
+                for g in range(rows // STEP)
+            ],
+            axis=1,
+        ).astype(BF16)
 
     @pl.when(jnp.logical_not(last))
     def _():
-        down_copy(n_out, n_in, n_sem).start()
-
-    pd_all[t] = pd[...].astype(BF16)
-    pn_all[t] = (pn[...] - probe_t[...] * pd[...]).astype(BF16)
-
-    def probe_copy(buffer, send, recv, step):
-        return pltpu.make_async_remote_copy(
-            src_ref=buffer.at[t],
-            dst_ref=buffer.at[t],
-            send_sem=send.at[step - 1],
-            recv_sem=recv.at[step - 1],
-            device_id=tile_id((t + step) % n_tile),
-            device_id_type=MESH,
-        )
-
-    for step in range(1, n_tile):
-        probe_copy(pd_all, pd_send, pd_recv, step).start()
-        probe_copy(pn_all, pn_send, pn_recv, step).start()
+        down_copy(rest_out, rest_in, n_sem.at[2], n_sem.at[3]).start()
 
     @pl.when(first)
     def _():
         n_in[...] = jnp.zeros_like(n_in)
+        rest_in[...] = jnp.zeros_like(rest_in)
         d_in[...] = jnp.zeros_like(d_in)
 
     @pl.when(jnp.logical_not(first))
     def _():
-        down_copy(d_out, d_in, d_sem).wait_recv()
-        down_copy(n_out, n_in, n_sem).wait_recv()
+        down_copy(d_out, d_in, d_sem.at[0], d_sem.at[1]).wait_recv()
+        down_copy(n_out, n_in, n_sem.at[0], n_sem.at[1]).wait_recv()
+        down_copy(rest_out, rest_in, n_sem.at[2], n_sem.at[3]).wait_recv()
 
     scale = 1.0 / (sum_d[0] + d_in[...].astype(F32) + floor_d)
     for plane in range(2):
         top = sum_n[plane, 0] - sum_d[0] * ext[plane, 0] + n_in[plane].astype(F32)
+        rest = rest_in[plane].astype(F32)
+        rest = jnp.concatenate(
+            [rest[:, g * STEP : (g + 1) * STEP] for g in range(rows // STEP)], axis=0
+        )
+        top += jnp.concatenate([rest, jnp.zeros((width, rows - STEP), F32)], axis=1)
         x_new[plane] = obj[plane] + top * scale
 
     for block in range(n_chan):
@@ -367,6 +400,22 @@
 
     for step in range(1, n_chan):
         chan_copy(a_out, a_in, a_send, a_recv, step).start()
+    pd_all[t] = pd[...].astype(BF16)
+    pn_all[t] = (pn[...] - probe_t[...] * pd[...]).astype(BF16)
+
+    def probe_copy(buffer, send, recv, step):
+        return pltpu.make_async_remote_copy(
+            src_ref=buffer.at[t],
+            dst_ref=buffer.at[t],
+            send_sem=send.at[step - 1],
+            recv_sem=recv.at[step - 1],
+            device_id=tile_id((t + step) % n_tile),
+            device_id_type=MESH,
+        )
+
+    for step in range(1, n_tile):
+        probe_copy(pd_all, pd_send, pd_recv, step).start()
+        probe_copy(pn_all, pn_send, pn_recv, step).start()
     a_in[me] = a_out[me]
     for i in range(5, 8):
         loads[i].wait()
@@ -415,12 +464,14 @@
 
     @pl.when(jnp.logical_not(first))
     def _():
-        halo_copy().wait_send()
+        halo_copy(0).wait_send()
+        halo_copy(1).wait_send()
 
     @pl.when(jnp.logical_not(last))
     def _():
-        down_copy(d_out, d_in, d_sem).wait_send()
-        down_copy(n_out, n_in, n_sem).wait_send()
+        down_copy(d_out, d_in, d_sem.at[0], d_sem.at[1]).wait_send()
+        down_copy(n_out, n_in, n_sem.at[0], n_sem.at[1]).wait_send()
+        down_copy(rest_out, rest_in, n_sem.at[2], n_sem.at[3]).wait_send()
 
     for step in range(1, n_tile):
         probe_copy(pd_all, pd_send, pd_recv, step).wait_send()
@@ -447,8 +498,8 @@
     out_obj, out_probe = pl.pallas_call(
         functools.partial(kernel, sizes),
         out_shape=(
-            jax.ShapeDtypeStruct((2, width, rows), F32),
-            jax.ShapeDtypeStruct((2, modes, extent, extent), F32),
+            pltpu.VMEM((2, width, rows), F32),
+            pltpu.VMEM((2, modes, extent, extent), F32),
         ),
         in_specs=[hbm] * 8,
         out_specs=(vmem, vmem),
@@ -472,12 +523,14 @@
             pltpu.VMEM((2, width, rows), F32),
             pltpu.VMEM((2, modes, extent, extent), F32),
             pltpu.VMEM((extent, extent), F32),
-            pltpu.VMEM((2, width, rows), BF16),
-            pltpu.VMEM((2, width, rows), BF16),
+            pltpu.VMEM((2, 2, width // 2, rows), BF16),
+            pltpu.VMEM((2, 2, width // 2, rows), BF16),
             pltpu.VMEM((width, rows), BF16),
             pltpu.VMEM((width, rows), BF16),
             pltpu.VMEM((2, width, rows), BF16),
             pltpu.VMEM((2, width, rows), BF16),
+            pltpu.VMEM((2, width // (rows // STEP), rows), BF16),
+            pltpu.VMEM((2, width // (rows // STEP), rows), BF16),
             pltpu.VMEM((n_tile, 2, modes, extent, extent), BF16),
             pltpu.VMEM((n_tile, extent, extent), BF16),
             pltpu.VMEM((2, width, rows), F32),
@@ -485,9 +538,9 @@
             pltpu.VMEM((n_chan, share, rows), BF16),
             pltpu.VMEM((n_chan, share, rows), BF16),
             pltpu.VMEM((n_chan, share, rows), BF16),
+            dma((4,)),
             dma((2,)),
-            dma((2,)),
-            dma((2,)),
+            dma((4,)),
             dma((peers,)),
             dma((peers,)),
             dma((peers,)),
@@ -498,7 +551,7 @@
             dma((n_chan - 1,)),
         ],
         compiler_params=pltpu.CompilerParams(
-            collective_id=0, has_side_effects=True, vmem_limit_bytes=40 * 1024 * 1024
+            collective_id=0, has_side_effects=True, vmem_limit_bytes=58 * 1024 * 1024
         ),
         cost_estimate=pl.CostEstimate(flops=flops, bytes_accessed=2000000, transcendentals=0),
     )(

time: 35.4 us -> 28.7 us (0.81)
  local copies, waits for them, and re-layouts: 6.5 us -> 1.42 us
  Pallas kernels: 27.9 us -> 26.5 us
    unnamed x18 -> x2, local copies, waits for them, and re-layouts: 6.5 us -> 1.42 us
    pallas_call x1, Pallas kernels: 27.9 us -> 26.5 us  [body(): pl.pallas_call(functools.partial(kernel, sizes), out_shape=(pltpu.VMEM((2...]
where the time goes in v2:
time: 28.7 us; the launch traced here: 28.5 us
  Pallas kernels  26.5 us (92%)
  local copies, waits for them, and re-layouts  1.42 us (5%)
  between operations  0.64 us (2%)
    pallas_call x1, Pallas kernels, body(): pl.pallas_call(functools.partial(kernel, sizes), out_shape=(pltpu.VMEM((2...  26.5 us
    unnamed x2, local copies, waits for them, and re-layouts  1.42 us

profile of v2, /device:TPU:3, one launch (start us, length us, event | category | flops | bytes accessed | tf_op | source)
XLA Modules:
  0.0 28.5 jit_solution(5496708447443275010)
XLA Ops:
  0.6 26.5 %shard_map.95 = (f32[2,192,128]{2,1,0:T(8,128)S(1)}, f32[2,3,128,128]{3,2,1,0:T(8,128)S(1)}) custom-call(s32[2,8]{1,0:T(2,128)} %bitcast.21, f32[8,8]{1,0:T(8,128)} %basis_hbm.1, f32[8,8]{1,0:T(8,128)} %analysis_hbm.1, f32[8]{0:T(128)} %thr_hbm.1, bf16[128,256]{1,0:T(8,128)(2,1)} %constant.2.clone.dft_hbm, f32[2,192,128]{2,1,0:T(8,128)} %bitcast.20, ...), custom_call_target="tpu_custom_call" | custom-call | flops 1610612736 | bytes 2000000 | tf_op jit(solution)/shard_map/pallas_call | solution.py:498
  27.1 0.7 %copy.15 = f32[2,1,128,192]{2,3,1,0:T(8,128)} copy(f32[2,1,128,192]{2,3,1,0:T(8,128)S(1)} %bitcast.17) | data formatting | bytes 393216
  27.8 0.7 %copy.16 = f32[2,3,1,128,128]{4,3,2,1,0:T(8,128)} copy(f32[2,3,1,128,128]{4,3,2,1,0:T(8,128)S(1)} %bitcast.16) | data formatting | bytes 786432

commit v3 on v2

--- a/solution.py
+++ b/solution.py
@@ -53,6 +53,7 @@
     fwd,
     bwd,
     probe_t,
+    mod_t,
     ext,
     power,
     place,
@@ -188,13 +189,13 @@
     power[...] = total
     floor_d = 0.1 * jnp.max(total) + 1e-06
     span = extent + STEP
+    lane = lax.broadcasted_iota(jnp.int32, (extent, rows), 1)
 
     def lay(plane, block, row):
-        moved = pltpu.roll(
-            jnp.concatenate([block, jnp.zeros((extent, rows), F32)], axis=1), row, axis=1
-        )
-        place[plane, 0, STEP : STEP + extent] = moved[:, :rows]
-        place[plane, 1, STEP : STEP + extent] = moved[:, rows:]
+        moved = pltpu.roll(block, row, axis=1)
+        inside = lane >= row
+        place[plane, 0, STEP : STEP + extent] = jnp.where(inside, moved, 0.0)
+        place[plane, 1, STEP : STEP + extent] = jnp.where(inside, 0.0, moved)
 
     loads[1].wait()
 
@@ -225,6 +226,12 @@
     bwd[extent:, :extent] = -sine
     loads[4].wait()
 
+    def turn(q, carry):
+        mod_t[q] = mod[q].astype(F32).T
+        return carry
+
+    lax.fori_loop(0, positions, turn, 0)
+
     def take_halo(part):
         halo_copy(part).wait_recv()
         packed = halo_in[part].astype(F32)
@@ -241,10 +248,11 @@
         ext[:, 1] = jnp.zeros((2, width, rows), F32)
 
     def window(plane, row, col):
-        both = jnp.concatenate(
-            [ext[plane, b, pl.ds(col, extent)] for b in range(2)], axis=1
-        )
-        return pltpu.roll(both, lax.rem(2 * rows - row, 2 * rows), axis=1)[:, :extent]
+        back = lax.rem(rows - row, rows)
+        here, below = (
+            pltpu.roll(ext[plane, b, pl.ds(col, extent)], back, axis=1) for b in range(2)
+        )
+        return jnp.where(lane < rows - row, here, below)
 
     def lanes_of(array, index):
         return array[:, index * extent : (index + 1) * extent]
@@ -265,14 +273,15 @@
             down_copy(n_out, n_in, n_sem.at[0], n_sem.at[1]).start()
 
     def one(i, carry):
-        k = lax.rem(i + 1, turns)
-
-        @pl.when(jnp.logical_and(i == 1, jnp.logical_not(last)))
-        def _():
-            take_halo(1)
-
-        @pl.when(i == turns - 1)
-        def _():
+        k = (i + 1) % turns
+
+        if i == min(1, turns - 1):
+
+            @pl.when(jnp.logical_not(last))
+            def _():
+                take_halo(1)
+
+        if i == turns - 1:
             send_most()
 
         objects, tall = [], []
@@ -289,50 +298,63 @@
                     ).astype(BF16)
                 )
         n_c = []
+        waves = range(PCOLS * modes)
+        half = dot(jnp.concatenate(tall, axis=0), bwd[...])
+        wide = jnp.concatenate(
+            [
+                jnp.concatenate(
+                    [rows_of(half, w)[:, :extent], rows_of(half, w)[:, extent:]], axis=0
+                )
+                for w in waves
+            ],
+            axis=1,
+        ).astype(BF16)
+        spec = dot(fwd[...], wide)
+        scaled = []
         for c in range(PCOLS):
-            half = dot(jnp.concatenate(tall[c * modes : (c + 1) * modes], axis=0), bwd[...])
-            wide = jnp.concatenate(
-                [
-                    jnp.concatenate(
-                        [rows_of(half, m)[:, :extent], rows_of(half, m)[:, extent:]], axis=0
-                    )
-                    for m in range(modes)
-                ],
-                axis=1,
-            ).astype(BF16)
-            spec = dot(fwd[...], wide)
-            squares = lanes_of(spec, 0) * lanes_of(spec, 0)
+            parts = [lanes_of(spec, c * modes + m) for m in range(modes)]
+            squares = parts[0] * parts[0]
             for m in range(1, modes):
-                squares += lanes_of(spec, m) * lanes_of(spec, m)
+                squares += parts[m] * parts[m]
             mag = squares[:extent] + squares[extent:]
-            factor = mod[k * PCOLS + c].astype(F32).T * lax.rsqrt(mag + 0.01)
+            factor = mod_t[k * PCOLS + c] * lax.rsqrt(mag + 0.01)
             both = jnp.concatenate([factor, factor], axis=0)
-            scaled = jnp.concatenate(
-                [(lanes_of(spec, m) * both).astype(BF16) for m in range(modes)], axis=1
-            )
-            ret = dot(bwd[...], scaled)
-            cols = jnp.concatenate(
-                [
-                    jnp.concatenate(
-                        [lanes_of(ret, m)[:extent], lanes_of(ret, m)[extent:]], axis=1
-                    )
-                    for m in range(modes)
-                ],
-                axis=0,
-            ).astype(BF16)
-            wave = dot(cols, fwd[...])
-            o_r, o_i = objects[c]
+            scaled += [(part * both).astype(BF16) for part in parts]
+        ret = dot(bwd[...], jnp.concatenate(scaled, axis=1))
+        cols = jnp.concatenate(
+            [
+                jnp.concatenate(
+                    [lanes_of(ret, w)[:extent], lanes_of(ret, w)[extent:]], axis=1
+                )
+                for w in waves
+            ],
+            axis=0,
+        ).astype(BF16)
+        wave = dot(cols, fwd[...])
+        for c in range(PCOLS):
             n_r = jnp.zeros((extent, extent), F32)
             n_i = jnp.zeros((extent, extent), F32)
             for m in range(modes):
                 p_r, p_i = probe_t[0, m], probe_t[1, m]
-                w_r, w_i = rows_of(wave, m)[:, :extent], rows_of(wave, m)[:, extent:]
+                got = rows_of(wave, c * modes + m)
+                w_r, w_i = got[:, :extent], got[:, extent:]
                 n_r += p_r * w_r + p_i * w_i
                 n_i += p_r * w_i - p_i * w_r
-                pn[0, m] += o_r * w_r + o_i * w_i
-                pn[1, m] += o_r * w_i - o_i * w_r
-            pd[...] += o_r * o_r + o_i * o_i
             n_c.append((n_r, n_i))
+        for m in range(modes):
+            pn_r, pn_i = pn[0, m], pn[1, m]
+            for c in range(PCOLS):
+                o_r, o_i = objects[c]
+                got = rows_of(wave, c * modes + m)
+                w_r, w_i = got[:, :extent], got[:, extent:]
+                pn_r += o_r * w_r + o_i * w_i
+                pn_i += o_r * w_i - o_i * w_r
+            pn[0, m] = pn_r
+            pn[1, m] = pn_i
+        weight = pd[...]
+        for o_r, o_i in objects:
+            weight += o_r * o_r + o_i * o_i
+        pd[...] = weight
         for c in range(PCOLS):
             q = k * PCOLS + c
             for plane in range(2):
@@ -346,7 +368,8 @@
                     ]
         return carry
 
-    lax.fori_loop(0, turns, one, 0)
+    for i in range(turns):
+        one(i, 0)
 
     for plane in range(2):
         rest_out[plane] = jnp.concatenate(
@@ -387,8 +410,16 @@
         at = slice(block * share, (block + 1) * share)
         a_out[block, :used] = jnp.concatenate([x_new[0, at], x_new[1, at]], axis=0).astype(BF16)
 
+    def peer(step):
+        other, bit = me, 1
+        while bit < n_chan:
+            if step & bit:
+                other = other + bit - 2 * bit * ((me // bit) % 2)
+            bit *= 2
+        return other
+
     def chan_copy(src, dst, send, recv, step):
-        other = (me + step) % n_chan
+        other = peer(step)
         return pltpu.make_async_remote_copy(
             src_ref=src.at[other],
             dst_ref=dst.at[me],
@@ -398,7 +429,7 @@
             device_id_type=MESH,
         )
 
-    for step in range(1, n_chan):
+    for step in range(n_chan - 1, 0, -1):
         chan_copy(a_out, a_in, a_send, a_recv, step).start()
     pd_all[t] = pd[...].astype(BF16)
     pn_all[t] = (pn[...] - probe_t[...] * pd[...]).astype(BF16)
@@ -416,29 +447,28 @@
     for step in range(1, n_tile):
         probe_copy(pd_all, pd_send, pd_recv, step).start()
         probe_copy(pn_all, pn_send, pn_recv, step).start()
-    a_in[me] = a_out[me]
     for i in range(5, 8):
         loads[i].wait()
+    spectrum = a_out[me].astype(F32)
+    total = [analysis[k, me] * spectrum for k in range(comps)]
     for step in range(1, n_chan):
         chan_copy(a_out, a_in, a_send, a_recv, step).wait_recv()
-
-    spectra = [a_in[e].astype(F32) for e in range(n_chan)]
-    shrunk = []
-    for k in range(comps):
-        c = analysis[k, 0] * spectra[0]
-        for e in range(1, n_chan):
-            c += analysis[k, e] * spectra[e]
-        limit = thr[k]
-        shrunk.append(c - jnp.minimum(jnp.maximum(c, -limit), limit))
-    for e in range(n_chan):
+        spectrum = a_in[peer(step)].astype(F32)
+        total = [total[k] + analysis[k, peer(step)] * spectrum for k in range(comps)]
+    shrunk = [
+        total[k] - jnp.minimum(jnp.maximum(total[k], -thr[k]), thr[k]) for k in range(comps)
+    ]
+
+    def project(e):
         x = basis[e, 0] * shrunk[0]
         for k in range(1, comps):
             x += basis[e, k] * shrunk[k]
-        b_out[e] = x.astype(BF16)
-
-    for step in range(1, n_chan):
+        return x.astype(BF16)
+
+    for step in range(n_chan - 1, 0, -1):
+        b_out[peer(step)] = project(peer(step))
         chan_copy(b_out, b_in, b_send, b_recv, step).start()
-    b_in[me] = b_out[me]
+    b_in[me] = project(me)
 
     for step in range(1, n_tile):
         probe_copy(pd_all, pd_send, pd_recv, step).wait_recv()
@@ -516,6 +546,7 @@
             pltpu.VMEM((2 * extent, 2 * extent), BF16),
             pltpu.VMEM((2 * extent, 2 * extent), BF16),
             pltpu.VMEM((2, modes, extent, extent), F32),
+            pltpu.VMEM((positions, extent, extent), F32),
             pltpu.VMEM((2, 2, width, rows), F32),
             pltpu.VMEM((extent, extent), F32),
             pltpu.VMEM((2 * PCOLS, 2, extent + 2 * STEP, rows), F32),

time: 28.7 us -> 26.1 us (0.909)
  Pallas kernels: 26.5 us -> 23.8 us
    pallas_call x1, Pallas kernels: 26.5 us -> 23.8 us  [body(): pl.pallas_call(functools.partial(kernel, sizes), out_shape=(pltpu.VMEM((2...]
where the time goes in v3:
time: 26.1 us; the launch traced here: 25.8 us
  Pallas kernels  23.8 us (91%)
  local copies, waits for them, and re-layouts  1.42 us (5%)
  between operations  0.64 us (2%)
    pallas_call x1, Pallas kernels, body(): pl.pallas_call(functools.partial(kernel, sizes), out_shape=(pltpu.VMEM((2...  23.8 us
    unnamed x2, local copies, waits for them, and re-layouts  1.42 us

profile of v3, /device:TPU:3, one launch (start us, length us, event | category | flops | bytes accessed | tf_op | source)
XLA Modules:
  0.0 25.8 jit_solution(4256671894533134161)
XLA Ops:
  0.6 23.8 %shard_map.95 = (f32[2,192,128]{2,1,0:T(8,128)S(1)}, f32[2,3,128,128]{3,2,1,0:T(8,128)S(1)}) custom-call(s32[2,8]{1,0:T(2,128)} %bitcast.21, f32[8,8]{1,0:T(8,128)} %basis_hbm.1, f32[8,8]{1,0:T(8,128)} %analysis_hbm.1, f32[8]{0:T(128)} %thr_hbm.1, bf16[128,256]{1,0:T(8,128)(2,1)} %constant.2.clone.dft_hbm, f32[2,192,128]{2,1,0:T(8,128)} %bitcast.20, ...), custom_call_target="tpu_custom_call" | custom-call | flops 1610612736 | bytes 2000000 | tf_op jit(solution)/shard_map/pallas_call | solution.py:528
  24.4 0.7 %copy.15 = f32[2,1,128,192]{2,3,1,0:T(8,128)} copy(f32[2,1,128,192]{2,3,1,0:T(8,128)S(1)} %bitcast.17) | data formatting | bytes 393216
  25.1 0.7 %copy.16 = f32[2,3,1,128,128]{4,3,2,1,0:T(8,128)} copy(f32[2,3,1,128,128]{4,3,2,1,0:T(8,128)S(1)} %bitcast.16) | data formatting | bytes 786432
